TPU v7x, 32 devices: a whole 2x2x4 slice. The times are simulated.
32 devices in a mesh: req: 8 (over y, x, core), blk: 4 (over z).
Axes of the slice: x: 2, y: 2, z: 4, core: 2. Of those that a mesh axis runs over, the one named last changes fastest.
Arguments:
- x_img: bfloat16 [8, 1024, 1536], P('req', 'blk'), may hold values from -0.3 to 0.3
- x_txt: bfloat16 [8, 154, 1536], P('req'), may hold values from -6 to 6
- modulation: float32 [8, 7, 1536], P('req'), may hold values from -8 to 8
- w_img: bfloat16 [1536, 2304], P(None, 'req'), may hold values from -0.375 to 0.375
- w_txt: bfloat16 [1536, 1536], P(None, 'req'), may hold values from -0.15625 to 0.15625
- w_out: bfloat16 [768, 1536], P('req'), may hold values from -0.21875 to 0.21875
- w_final: bfloat16 [1536, 64], replicated, may hold values from -0.15625 to 0.15625
- lengths: int32 [8], P('req'), may hold values from 16 to 154, as said below
- block_mask: int32 [8, 4, 4], P('req', 'blk'), may hold values from 0 to 1, as said below
- timestep: int32 [8], P('req'), may hold values from 0 to 27
- latent: float32 [8, 16, 32, 128], P('req', None, 'blk'), may hold values from -6 to 6
- conv_w: bfloat16 [512, 144], replicated, may hold values from -0.5 to 0.5
Outputs:
- velocity: float32 [8, 16, 32, 128], P('req', None, 'blk')
- latent_next: float32 [8, 16, 32, 128], P('req', None, 'blk')
- features: bfloat16 [8, 512, 32, 128], P('req', None, 'blk')
Inputs may be any that keep to these rules, and one draw needn't show every extreme that they name: Text keys from position lengths[r] on are padding; some request uses all 154 text tokens. Every tile may attend to its own keys: block_mask[r, t, t] = 1.
All inputs are finite; a program needn't handle non-finite values.
Results may differ from a plain program's by a relative error of at most 0.0063.
Values may be sent and summed in bfloat16 or wider, within the bound.
A program may use at most 192 MiB of HBM per device.

v0:
```python
import jax
import jax.numpy as jnp
from jax import lax
from jax.sharding import PartitionSpec as P

HD = 64
GRIDW = 64
PATCH = 2
LATC = 16
NSTEPS = 28
NORM_EPS = 1e-06
SHIFT_FACTOR = 3.0
LATENT_SCALE = 1.5305
LATENT_SHIFT = 0.0609
NEG_LARGE = -1e30
SCORE_SCALE = 0.125


def with_halo(block, sides, width):
    for axis, dim in sides:
        count = lax.axis_size(axis)
        forward = [(i, i + 1) for i in range(count - 1)]
        backward = [(target, source) for source, target in forward]
        low = lax.ppermute(
            lax.slice_in_dim(block, block.shape[dim] - width, None, axis=dim), axis, forward
        )
        high = lax.ppermute(lax.slice_in_dim(block, 0, width, axis=dim), axis, backward)
        block = jnp.concatenate([low, block, high], axis=dim)
    return block


def layer_norm(values):
    values = values.astype(jnp.float32)
    center = values - jnp.mean(values, axis=-1, keepdims=True)
    spread = jnp.mean(center * center, axis=-1, keepdims=True)
    return center * lax.rsqrt(spread + NORM_EPS)


def modulate(values, shift_row, scale_row):
    return layer_norm(values) * (1.0 + scale_row) + shift_row


def sigma_of(step_index, step_count):
    fraction = 1.0 - step_index.astype(jnp.float32) / step_count
    return SHIFT_FACTOR * fraction / (1.0 + (SHIFT_FACTOR - 1.0) * fraction)


def unpatchify(token_out, grid_width, patch_size, channels):
    patch_rows = token_out.shape[0] // grid_width
    shaped = token_out.reshape(patch_rows, grid_width, patch_size, patch_size, channels)
    shaped = jnp.transpose(shaped, (4, 0, 2, 1, 3))
    return shaped.reshape(channels, patch_rows * patch_size, grid_width * patch_size)


def convolve(padded, conv_w):
    row_count = padded.shape[1] - 2
    col_count = padded.shape[2] - 2
    tap_list = [
        padded[:, tap_row : tap_row + row_count, tap_col : tap_col + col_count]
        for tap_row in range(3)
        for tap_col in range(3)
    ]
    stacked = jnp.stack(tap_list, axis=1).reshape(padded.shape[0] * 9, row_count * col_count)
    convolved = jnp.dot(conv_w, stacked, preferred_element_type=jnp.float32)
    return convolved.reshape(conv_w.shape[0], row_count, col_count)


def text_state(queries, keys_txt, vals_txt, length):
    text_allowed = (jnp.arange(keys_txt.shape[0], dtype=jnp.int32) < length)[None, None, :]
    text_scores = (
        jnp.einsum("qhd,khd->qhk", queries, keys_txt, preferred_element_type=jnp.float32)
        * SCORE_SCALE
    )
    text_scores = jnp.where(text_allowed, text_scores, NEG_LARGE)
    text_max = jnp.max(text_scores, axis=2)
    text_weights = jnp.where(text_allowed, jnp.exp(text_scores - text_max[:, :, None]), 0.0)
    text_acc = jnp.einsum(
        "qhk,khd->qhd",
        text_weights.astype(jnp.bfloat16),
        vals_txt,
        preferred_element_type=jnp.float32,
    )
    return (text_max, jnp.sum(text_weights, axis=2), text_acc)


def absorb_block(previous, queries, head_keys, head_vals, allowed):
    old_max, old_sum, old_acc = previous
    scores = (
        jnp.einsum("qhd,khd->qhk", queries, head_keys, preferred_element_type=jnp.float32)
        * SCORE_SCALE
    )
    scores = jnp.where(allowed, scores, NEG_LARGE)
    new_max = jnp.maximum(old_max, jnp.max(scores, axis=2))
    weights = jnp.where(allowed, jnp.exp(scores - new_max[:, :, None]), 0.0)
    factor = jnp.exp(old_max - new_max)
    summed = jnp.einsum(
        "qhk,khd->qhd", weights.astype(jnp.bfloat16), head_vals, preferred_element_type=jnp.float32
    )
    return (
        new_max,
        old_sum * factor + jnp.sum(weights, axis=2),
        old_acc * factor[:, :, None] + summed,
    )


def absorb_maybe(previous, queries, head_keys, head_vals, allowed):
    return absorb_block(previous, queries, head_keys, head_vals, allowed)


def on_device(
    x_img,
    x_txt,
    modulation,
    w_img,
    w_txt,
    w_out,
    w_final,
    lengths,
    block_mask,
    timestep,
    latent,
    conv_w,
):
    tokens = x_img[0]
    factors = modulation[0]
    tok_rows = tokens.shape[0]
    head_cols = w_out.shape[0] * lax.axis_size("req")
    head_count = head_cols // HD
    h_img = modulate(tokens, factors[0], factors[1]).astype(jnp.bfloat16)
    h_txt = modulate(x_txt[0], factors[3], factors[4]).astype(jnp.bfloat16)
    qkv = jnp.dot(
        h_img, lax.all_gather(w_img, "req", axis=1, tiled=True), preferred_element_type=jnp.float32
    ).astype(jnp.bfloat16)
    kv_txt = jnp.dot(
        h_txt, lax.all_gather(w_txt, "req", axis=1, tiled=True), preferred_element_type=jnp.float32
    ).astype(jnp.bfloat16)
    keys_txt = kv_txt[:, :head_cols].reshape(-1, head_count, HD)
    vals_txt = kv_txt[:, head_cols:].reshape(-1, head_count, HD)
    length = lengths[0]
    queries = qkv[:, :head_cols].reshape(tok_rows, head_count, HD)
    keys_img = qkv[:, head_cols : 2 * head_cols]
    vals_img = qkv[:, 2 * head_cols :]
    mask_row = block_mask[0, 0]
    tile_count = mask_row.shape[0]
    start_state = text_state(queries, keys_txt, vals_txt, length)
    piece_keys = lax.all_gather(keys_img, "blk", axis=0, tiled=True)
    piece_vals = lax.all_gather(vals_img, "blk", axis=0, tiled=True)
    piece_len = piece_keys.shape[0]
    key_tile = jnp.arange(piece_len, dtype=jnp.int32) // tok_rows
    tile_hit = key_tile[:, None] == jnp.arange(tile_count, dtype=jnp.int32)[None, :]
    allowed = jnp.sum(jnp.where(tile_hit, mask_row[None, :], 0), axis=1) == 1
    head_keys = piece_keys.reshape(piece_len, head_count, HD)
    head_vals = piece_vals.reshape(piece_len, head_count, HD)
    run_max, run_sum, run_acc = absorb_maybe(
        start_state, queries, head_keys, head_vals, allowed[None, None, :]
    )
    attended = (run_acc / run_sum[:, :, None]).reshape(tok_rows, head_cols).astype(jnp.bfloat16)
    projected = jnp.dot(
        attended,
        lax.all_gather(w_out, "req", axis=0, tiled=True),
        preferred_element_type=jnp.float32,
    )
    residual = tokens.astype(jnp.float32) + factors[2] * projected
    final_in = modulate(residual, factors[5], factors[6]).astype(jnp.bfloat16)
    token_out = jnp.dot(final_in, w_final, preferred_element_type=jnp.float32)
    velocity = unpatchify(token_out, GRIDW, PATCH, LATC)[None]
    step_index = timestep[0]
    sigma_step = sigma_of(step_index + 1, NSTEPS) - sigma_of(step_index, NSTEPS)
    latent_next = latent + sigma_step * velocity
    decoded = (latent_next / LATENT_SCALE + LATENT_SHIFT).astype(jnp.bfloat16)
    padded = with_halo(decoded, (("blk", 2),), 1)
    padded = jnp.pad(padded[0], ((0, 0), (0, 0), (1, 1)))
    features = convolve(padded, conv_w).astype(jnp.bfloat16)[None]
    return (velocity, latent_next, features)


def solution(mesh):
    return jax.shard_map(
        on_device,
        mesh=mesh,
        in_specs=(
            P("req", "blk", None),
            P("req", None, None),
            P("req", None, None),
            P(None, "req"),
            P(None, "req"),
            P("req", None),
            P(),
            P("req"),
            P("req", "blk", None),
            P("req"),
            P("req", None, "blk", None),
            P(),
        ),
        out_specs=(
            P("req", None, "blk", None),
            P("req", None, "blk", None),
            P("req", None, "blk", None),
        ),
        check_vma=False,
    )
```

profile of v0, /device:TPU:0, one launch (start us, length us, event | category | flops | bytes accessed | tf_op | source)
XLA Modules:
  0.0 230.1 jit_solution(16971153236048344387)
XLA Ops:
  7.2 0.0 copy-start
  7.2 0.0 all-gather.8.cloned.1.call-start
  7.2 0.7 all-gather.8.cloned.1.call-update
  7.9 0.0 all-gather.6.cloned.1.call-start
  8.0 0.7 all-gather.6.cloned.1.call-update
  8.7 0.0 all-gather.10.cloned.1.call-start
  8.7 0.9 add_reduce_fusion
  9.6 0.0 copy-done.2
  9.6 0.2 convert_reduce_fusion
  9.8 0.3 fusion.14
  10.2 51.3 %all-gather.8.cloned.1.call-done = bf16[1536,2304]{0,1:T(8,128)(2,1)} async-done(((bf16[1536,288]{0,1:T(8,128)(2,1)}), bf16[1536,2304]{0,1:T(8,128)(2,1)}) %all-gather.8.cloned.1.call-update) | async-done | bytes 7077904 | tf_op jit(solution)/shard_map/all_gather | solution.py:132
  61.5 5.2 %convolution_convert_fusion = bf16[256,2304]{1,0:T(8,128)(2,1)S(1)} fusion(bf16[1536,2304]{0,1:T(8,128)(2,1)} %all-gather.8.cloned.1.call-done, bf16[1,256,1536]{2,1,0:T(8,128)(2,1)S(1)} %copy-done.2, f32[1536]{0:T(1024)S(1)} %get-tuple-element.16, f32[1536]{0:T(1024)S(1)} %get-tuple-element.17, f32[256]{0:T(256)S(1)} %add_rsqrt_fusion.1, ...), kind=kOutput, calls=%fused_computation.10 | convolution fusion | flops 1814888448 | bytes 9058304 | tf_op jit(solution)/shard_map/dot_general | solution.py:131
  66.7 0.0 copy-start.4
  66.7 0.0 copy-start.8
  66.7 0.0 copy-start.7
  66.7 1.0 fusion.69
  67.7 0.0 all-gather.10.cloned.1.call-update
  67.7 0.0 all-gather.12.cloned.1.call-start
  67.7 0.5 all-gather.12.cloned.1.call-update
  68.3 0.0 all-gather.14.cloned.1.call-start
  68.3 0.5 all-gather.14.cloned.1.call-update
  69.5 0.1 convert_reduce_fusion.1
  69.7 0.3 fusion.30
  70.7 0.0 copy-done.8
  70.7 0.1 select_reduce_fusion
  70.8 1.0 copy.66
  71.9 30.4 %all-gather.6.cloned.1.call-done = bf16[1536,1536]{0,1:T(8,128)(2,1)} async-done(((bf16[1536,192]{0,1:T(8,128)(2,1)}), bf16[1536,1536]{0,1:T(8,128)(2,1)}) %all-gather.6.cloned.1.call-update) | async-done | bytes 4718608 | tf_op jit(solution)/shard_map/all_gather | solution.py:135
  102.3 4.0 %convolution_convert_fusion.1 = bf16[154,1536]{1,0:T(8,128)(2,1)S(1)} fusion(bf16[1536,1536]{0,1:T(8,128)(2,1)} %all-gather.6.cloned.1.call-done, bf16[1,154,1536]{2,1,0:T(8,128)(2,1)S(1)} %copy-done.4, f32[1536]{0:T(1024)S(1)} %get-tuple-element.18, f32[1536]{0:T(1024)S(1)} %get-tuple-element.19, f32[154]{0:T(256)S(1)} %add_rsqrt_fusion.2, ...), kind=kOutput, calls=%fused_computation.13 | convolution fusion | flops 728318976 | bytes 5678288 | tf_op jit(solution)/shard_map/dot_general | solution.py:134
  106.4 0.9 copy.60
  107.3 0.9 copy.59
  108.3 0.2 copy.61
  108.4 1.6 bitcast_reduce_fusion.1
  110.0 0.6 fusion.18
  110.6 30.5 %all-gather.10.cloned.1.call-done = bf16[1024,768]{1,0:T(8,128)(2,1)} async-done(((bf16[256,768]{1,0:T(8,128)(2,1)}), bf16[1024,768]{1,0:T(8,128)(2,1)}) %all-gather.10.cloned.1.call-update) | async-done | bytes 1572880 | tf_op jit(solution)/shard_map/all_gather | solution.py:146
  141.0 2.6 %copy.62 = bf16[1024,768]{0,1:T(8,128)(2,1)} copy(bf16[1024,768]{1,0:T(8,128)(2,1)} %all-gather.10.cloned.1.call-done) | data formatting | bytes 3145728 | tf_op jit(solution)/shard_map/all_gather | solution.py:146
  143.6 8.8 %bitcast_reduce_fusion = (f32[256,12]{0,1:T(8,128)S(1)}, f32[12,1024,256]{2,1,0:T(8,128)}) fusion(pred[1024]{0:T(1024)(128)(4,1)S(1)} %broadcast_compare_fusion, bf16[1024,12,64]{0,2,1:T(8,128)(2,1)} %bitcast.129, bf16[256,12,64]{0,2,1:T(8,128)(2,1)S(1)} %bitcast.134), kind=kOutput, calls=%fused_computation.1 | convolution fusion | flops 412087296 | bytes 14562304 | tf_op jit(solution)/shard_map/qhd,khd->qhk/dot_general | solution.py:89
  152.5 26.0 %all-gather.12.cloned.1.call-done = bf16[1024,768]{1,0:T(8,128)(2,1)} async-done(((bf16[256,768]{1,0:T(8,128)(2,1)}), bf16[1024,768]{1,0:T(8,128)(2,1)}) %all-gather.12.cloned.1.call-update) | async-done | bytes 1572880 | tf_op jit(solution)/shard_map/all_gather | solution.py:147
  178.4 2.6 %copy.63 = bf16[1024,768]{0,1:T(8,128)(2,1)} copy(bf16[1024,768]{1,0:T(8,128)(2,1)} %all-gather.12.cloned.1.call-done) | data formatting | bytes 3145728 | tf_op jit(solution)/shard_map/all_gather | solution.py:147
  181.0 7.2 %fusion.2 = f32[256,12]{0,1:T(8,128)S(1)} fusion(f32[12,1024,256]{2,1,0:T(8,128)} %get-tuple-element.45, f32[256,12]{0,1:T(8,128)S(1)} %max.13, pred[1024]{0:T(1024)(128)(4,1)S(1)} %broadcast_compare_fusion), kind=kLoop, calls=%fused_computation.5 | loop fusion | flops 15725568 | bytes 12608512 | tf_op jit(solution)/shard_map/reduce_sum | solution.py:101
  188.3 1.3 copy-done.1
  189.6 4.3 %fusion.20 = f32[256,12,64]{0,2,1:T(8,128)S(1)} fusion(bf16[1024,12,64]{0,2,1:T(8,128)(2,1)} %bitcast.135, f32[12,1024,256]{2,1,0:T(8,128)S(1)} %copy-done.1, f32[256,12]{0,1:T(8,128)S(1)} %max.13, pred[1024]{0:T(1024)(128)(4,1)S(1)} %broadcast_compare_fusion), kind=kOutput, calls=%fused_computation.33 | convolution fusion | flops 418381824 | bytes 14955520 | tf_op jit(solution)/shard_map/qhk,khd->qhd/dot_general | solution.py:96
  193.9 0.0 copy-done.5
  193.9 0.7 fusion.26
  194.6 13.5 %all-gather.14.cloned.1.call-done = bf16[768,1536]{1,0:T(8,128)(2,1)} async-done(((bf16[96,1536]{1,0:T(8,128)(2,1)}), bf16[768,1536]{1,0:T(8,128)(2,1)}) %all-gather.14.cloned.1.call-update) | async-done | bytes 2359312 | tf_op jit(solution)/shard_map/all_gather | solution.py:160
  208.1 2.5 %fusion.72 = (f32[256]{0:T(256)S(1)}, f32[256,1536]{1,0:T(8,128)S(1)}) fusion(bf16[256,768]{0,1:T(8,128)(2,1)S(1)} %bitcast.137, bf16[768,1536]{1,0:T(8,128)(2,1)} %all-gather.14.cloned.1.call-done, f32[1536]{0:T(1024)S(1)} %get-tuple-element.20, bf16[1,256,1536]{2,1,0:T(8,128)(2,1)S(1)} %copy-done.2), kind=kOutput, calls=%fused_computation.127 | convolution fusion | flops 605552384 | bytes 5118976 | tf_op jit(solution)/shard_map/dot_general | solution.py:158
  210.6 0.0 copy-start.3
  210.6 0.3 multiply_reduce_fusion
  211.0 0.5 fusion.46
  211.4 0.1 reshape.190
  211.6 0.3 copy.65
  211.8 0.0 copy-start.6
  211.9 0.1 add_convert_fusion.2
  212.0 3.4 %collective-permute-start = (bf16[1,16,1,128]{1,3,2,0:T(8,128)(2,1)S(1)}, bf16[1,16,1,128]{1,3,2,0:T(8,128)(2,1)S(1)}, u32[]{:S(2)}, u32[]{:S(2)}) collective-permute-start(bf16[1,16,1,128]{1,3,2,0:T(8,128)(2,1)S(1)} %get-tuple-element.31), channel_id=1, source_target_pairs={{0,1},{1,2},{2,3},{4,5},{5,6},{6,7},{8,9},{9,10},{10,11},{12,13},{... | collective-permute-start | bytes 12296 | tf_op jit(solution)/shard_map/ppermute | solution.py:24
  215.4 1.3 collective-permute-start.1
  216.7 0.1 copy.68
  216.8 0.8 copy.79
  217.6 0.8 copy.80
  218.4 0.0 collective-permute-done
  218.4 0.1 copy.67
  218.5 2.7 %collective-permute-done.1 = bf16[1,16,1,128]{1,3,2,0:T(8,128)(2,1)S(1)} collective-permute-done((bf16[1,16,1,128]{1,3,2,0:T(8,128)(2,1)S(1)}, bf16[1,16,1,128]{1,3,2,0:T(8,128)(2,1)S(1)}, u32[]{:S(2)}, u32[]{:S(2)}) %collective-permute-start.1) | collective-permute-done | bytes 4128 | tf_op jit(solution)/shard_map/ppermute | solution.py:27
  221.2 0.1 copy.69
  221.3 0.1 fusion.59
  221.6 0.5 convolution_convert_fusion.2
  222.1 1.5 copy.81
  (31 shorter events, 0.3 us)
Async XLA Ops:
  7.2 203.8 %copy-start = (bf16[1536,64]{0,1:T(8,128)(2,1)S(1)}, bf16[1536,64]{0,1:T(8,128)(2,1)}, u32[]{:S(2)}) copy-start(bf16[1536,64]{0,1:T(8,128)(2,1)} %param.18) | copy-start | bytes 589828
  7.2 2.5 %copy-start.2 = (bf16[1,256,1536]{2,1,0:T(8,128)(2,1)S(1)}, bf16[1,256,1536]{2,1,0:T(8,128)(2,1)}, u32[]{:S(2)}) copy-start(bf16[1,256,1536]{2,1,0:T(8,128)(2,1)} %param.12) | copy-start | bytes 2359300
  7.2 54.3 %all-gather.8.cloned.1.call-start = ((), (), s32[]{:S(2)}) async-start(), calls=%async_computation.1 | async-start | bytes 7962624 | tf_op jit(solution)/shard_map/all_gather | solution.py:132
  7.9 94.4 %all-gather.6.cloned.1.call-start = ((), (), s32[]{:S(2)}) async-start(), calls=%async_computation | async-start | bytes 5308416 | tf_op jit(solution)/shard_map/all_gather | solution.py:135
  8.7 132.4 %all-gather.10.cloned.1.call-start = ((), (), s32[]{:S(2)}) async-start(), calls=%async_computation.2 | async-start | bytes 1966080 | tf_op jit(solution)/shard_map/all_gather | solution.py:146
  66.7 2.9 %copy-start.4 = (bf16[1,154,1536]{2,1,0:T(8,128)(2,1)S(1)}, bf16[1,154,1536]{2,1,0:T(8,128)(2,1)}, u32[]{:S(2)}) copy-start(bf16[1,154,1536]{2,1,0:T(8,128)(2,1)} %param.13) | copy-start | bytes 1419268
  66.7 4.0 %copy-start.8 = (s32[1,1,4]{2,1,0:T(1,128)S(1)}, s32[1,1,4]{2,1,0:T(1,128)}, u32[]{:S(2)}) copy-start(s32[1,1,4]{2,1,0:T(1,128)} %param.20) | copy-start | bytes 52
  66.7 4.1 %copy-start.7 = (f32[1,16,8,128]{3,2,1,0:T(8,128)S(1)}, f32[1,16,8,128]{3,2,1,0:T(8,128)}, u32[]{:S(2)}) copy-start(f32[1,16,8,128]{3,2,1,0:T(8,128)} %param.22) | copy-start | bytes 196612
  67.7 110.8 %all-gather.12.cloned.1.call-start = ((), (), s32[]{:S(2)}) async-start(), calls=%async_computation.3 | async-start | bytes 1966080 | tf_op jit(solution)/shard_map/all_gather | solution.py:147
  68.3 139.8 %all-gather.14.cloned.1.call-start = ((), (), s32[]{:S(2)}) async-start(), calls=%async_computation.4 | async-start | bytes 2654208 | tf_op jit(solution)/shard_map/all_gather | solution.py:160
  181.0 8.5 %copy-start.1 = (f32[12,1024,256]{2,1,0:T(8,128)S(1)}, f32[12,1024,256]{2,1,0:T(8,128)}, u32[]{:S(2)}) copy-start(f32[12,1024,256]{2,1,0:T(8,128)} %get-tuple-element.45) | copy-start | bytes 37748740
  189.6 4.3 %copy-start.5 = (bf16[154,768]{0,1:T(8,128)(2,1)S(1)}, bf16[154,768]{0,1:T(8,128)(2,1)}, u32[]{:S(2)}) copy-start(bf16[154,768]{0,1:T(8,128)(2,1)} %copy.59) | copy-start | bytes 709636
  210.6 1.2 copy-start.3
  211.8 9.8 %copy-start.6 = (bf16[512,144]{0,1:T(8,128)(2,1)S(1)}, bf16[512,144]{0,1:T(8,128)(2,1)}, u32[]{:S(2)}) copy-start(bf16[512,144]{0,1:T(8,128)(2,1)} %param.23) | copy-start | bytes 442372
  212.0 6.4 %collective-permute-start = (bf16[1,16,1,128]{1,3,2,0:T(8,128)(2,1)S(1)}, bf16[1,16,1,128]{1,3,2,0:T(8,128)(2,1)S(1)}, u32[]{:S(2)}, u32[]{:S(2)}) collective-permute-start(bf16[1,16,1,128]{1,3,2,0:T(8,128)(2,1)S(1)} %get-tuple-element.31), channel_id=1, source_target_pairs={{0,1},{1,2},{2,3},{4,5},{5,6},{6,7},{8,9},{9,10},{10,11},{12,13},{... | collective-permute-start | bytes 12296 | tf_op jit(solution)/shard_map/ppermute | solution.py:24
  215.4 5.8 %collective-permute-start.1 = (bf16[1,16,1,128]{1,3,2,0:T(8,128)(2,1)S(1)}, bf16[1,16,1,128]{1,3,2,0:T(8,128)(2,1)S(1)}, u32[]{:S(2)}, u32[]{:S(2)}) collective-permute-start(bf16[1,16,1,128]{1,3,2,0:T(8,128)(2,1)S(1)} %get-tuple-element.32), channel_id=1, source_target_pairs={{1,0},{2,1},{3,2},{5,4},{6,5},{7,6},{9,8},{10,9},{11,10},{13,12},{... | collective-permute-start | bytes 12296 | tf_op jit(solution)/shard_map/ppermute | solution.py:27
Sparse Core Ops, SparseCore 0:
  9.9 51.5 all-gather.7
  63.4 38.9 all-gather.5
  103.9 37.0 all-gather.9
  142.5 35.9 all-gather.11
  180.2 27.8 all-gather.13
where the time goes:
time: 231 us; the launch traced here: 230 us
  waiting for transfers between devices  157 us (68%)
  matrix products  28 us (12%)
  between operations  15.5 us (7%)
  local copies, waits for them, and re-layouts  14.5 us (6%)
  other arithmetic  10.2 us (4%)
  starting transfers between devices  4.88 us (2%)
    all_gather x1, waiting for transfers between devices, on_device(): lax.all_gather(w_img, 'req', axis=1, tiled=True)  51.3 us
    all_gather x1, waiting for transfers between devices, on_device(): piece_keys = lax.all_gather(keys_img, 'blk', axis=0, tiled=True)  30.5 us
    all_gather x1, waiting for transfers between devices, on_device(): lax.all_gather(w_txt, 'req', axis=1, tiled=True)  30.4 us
    all_gather x1, waiting for transfers between devices, on_device(): piece_vals = lax.all_gather(vals_img, 'blk', axis=0, tiled=True)  26 us
    all_gather x1, waiting for transfers between devices, on_device(): lax.all_gather(w_out, 'req', axis=0, tiled=True)  13.5 us
    dot_general x1, matrix products, absorb_block(): jnp.einsum('qhd,khd->qhk', queries, head_keys, preferred_element_type=jnp...  8.82 us
    reduce_sum x1, other arithmetic, absorb_block(): jnp.sum(weights, axis=2)  7.21 us
    unnamed x30, local copies, waits for them, and re-layouts  5.57 us
  transfers between devices with their start and end apart: 7, of which 6 were waited for; matrix products, arithmetic and copies ran while one was open for 20% of the time, Pallas kernels for 0%

commit v1 on v0

--- a/solution.py
+++ b/solution.py
@@ -143,7 +143,31 @@
     mask_row = block_mask[0, 0]
     tile_count = mask_row.shape[0]
     start_state = text_state(queries, keys_txt, vals_txt, length)
-    piece_keys = lax.all_gather(keys_img, "blk", axis=0, tiled=True)
+    z_new = lax.axis_size("blk")
+    local_part = lax.axis_index("blk")
+    wide_out, field_out, everything = (z_new, local_part, keys_img.shape[0])
+    panels = tuple(((m, (m + 1) % wide_out) for m in range(wide_out)))
+    by_rank = tuple(((m, (m - 1) % wide_out) for m in range(wide_out)))
+    piece_keys = jnp.zeros(
+        (*keys_img.shape[:0], wide_out * everything, *keys_img.shape[1:]), keys_img.dtype
+    )
+    then = e_now = keys_img
+    carry = wide_out // 2
+    b = 1
+    piece_keys = lax.dynamic_update_slice_in_dim(
+        piece_keys, keys_img, field_out * everything, axis=0
+    )
+    while b < carry + 1:
+        then = lax.ppermute(then, axis_name="blk", perm=panels)
+        piece_keys = lax.dynamic_update_slice_in_dim(
+            piece_keys, then, (field_out - b) % wide_out * everything, axis=0
+        )
+        if b < wide_out - carry:
+            e_now = lax.ppermute(e_now, perm=by_rank, axis_name="blk")
+            piece_keys = lax.dynamic_update_slice_in_dim(
+                piece_keys, e_now, (field_out + b) % wide_out * everything, axis=0
+            )
+        b += 1
     piece_vals = lax.all_gather(vals_img, "blk", axis=0, tiled=True)
     piece_len = piece_keys.shape[0]
     key_tile = jnp.arange(piece_len, dtype=jnp.int32) // tok_rows

time: 231 us -> 214 us (0.926)
  waiting for transfers between devices: 157 us -> 118 us
  starting transfers between devices: 4.88 us -> 18.3 us
  local copies, waits for them, and re-layouts: 14.5 us -> 27.9 us
  other arithmetic: 10.2 us -> 6.59 us
    all_gather x1 -> x0, waiting for transfers between devices: 30.5 us -> none  [on_device(): piece_keys = lax.all_gather(keys_img, 'blk', axis=0, tiled=True)]
    all_gather x1, waiting for transfers between devices: 26 us -> 0.02 us  [on_device(): piece_vals = lax.all_gather(vals_img, 'blk', axis=0, tiled=True)]
    ppermute x0 -> x3, waiting for transfers between devices: none -> 21.2 us  [the longest x2 13.4 us: on_device(): then = lax.ppermute(then, axis_name='blk', perm=panels)]
    ppermute x0 -> x3, starting transfers between devices: none -> 13.5 us  [the longest x2 11.2 us: on_device(): then = lax.ppermute(then, axis_name='blk', perm=panels)]
    dynamic_update_slice x0 -> x4, local copies, waits for them, and re-layouts: none -> 7.21 us  [the longest x2 3.61 us: on_device(): lax.dynamic_update_slice_in_dim(piece_keys, then, (field_out - b) % wide_...]
    ppermute x0 -> x3, local copies, waits for them, and re-layouts: none -> 5.78 us  [the longest x2 3.85 us: on_device(): then = lax.ppermute(then, axis_name='blk', perm=panels)]
    dot_general x1, matrix products: 8.82 us -> 4.23 us  [absorb_block(): jnp.einsum('qhd,khd->qhk', queries, head_keys, preferred_element_type=jnp...]
    all_gather x1, waiting for transfers between devices: 13.5 us -> 9.37 us  [on_device(): lax.all_gather(w_out, 'req', axis=0, tiled=True)]
  transfers between devices with their start and end apart: 7 -> 9, of which waited for: 6 -> 7; matrix products, arithmetic and copies ran while one was open for 20% -> 26% of each run, Pallas kernels for 0% -> 0%
where the time goes in v1:
time: 214 us; the launch traced here: 213 us
  waiting for transfers between devices  118 us (55%)
  local copies, waits for them, and re-layouts  27.9 us (13%)
  matrix products  27 us (13%)
  starting transfers between devices  18.3 us (9%)
  between operations  15.6 us (7%)
  other arithmetic  6.59 us (3%)
    all_gather x1, waiting for transfers between devices, on_device(): lax.all_gather(w_img, 'req', axis=1, tiled=True)  51.3 us
    all_gather x1, waiting for transfers between devices, on_device(): lax.all_gather(w_txt, 'req', axis=1, tiled=True)  31 us
    ppermute x2, waiting for transfers between devices, on_device(): then = lax.ppermute(then, axis_name='blk', perm=panels)  13.4 us
    ppermute x2, starting transfers between devices, on_device(): then = lax.ppermute(then, axis_name='blk', perm=panels)  11.2 us
    all_gather x1, waiting for transfers between devices, on_device(): lax.all_gather(w_out, 'req', axis=0, tiled=True)  9.37 us
    dot_general x1, matrix products, absorb_block(): jnp.einsum('qhk,khd->qhd', weights.astype(jnp.bfloat16), head_vals, prefe...  7.82 us
    ppermute x1, waiting for transfers between devices, on_device(): e_now = lax.ppermute(e_now, perm=by_rank, axis_name='blk')  7.78 us
    unnamed x30, local copies, waits for them, and re-layouts  5.23 us
  transfers between devices with their start and end apart: 9, of which 7 were waited for; matrix products, arithmetic and copies ran while one was open for 26% of the time, Pallas kernels for 0%

profile of v1, /device:TPU:0, one launch (start us, length us, event | category | flops | bytes accessed | tf_op | source)
XLA Modules:
  0.0 213.0 jit_solution(4402754046131051732)
XLA Ops:
  7.2 0.0 all-gather.7.cloned.1.call-start
  7.2 0.7 all-gather.7.cloned.1.call-update
  7.9 0.0 all-gather.5.cloned.1.call-start
  8.0 0.7 all-gather.5.cloned.1.call-update
  8.7 0.0 all-gather.9.cloned.1.call-start
  8.7 0.9 add_reduce_fusion
  9.6 0.2 convert_reduce_fusion
  9.8 0.3 fusion.14
  10.2 51.3 %all-gather.7.cloned.1.call-done = bf16[1536,2304]{0,1:T(8,128)(2,1)} async-done(((bf16[1536,288]{0,1:T(8,128)(2,1)}), bf16[1536,2304]{0,1:T(8,128)(2,1)}) %all-gather.7.cloned.1.call-update) | async-done | bytes 7077904 | tf_op jit(solution)/shard_map/all_gather | solution.py:132
  61.5 5.2 %convolution_convert_fusion = bf16[256,2304]{1,0:T(8,128)(2,1)S(1)} fusion(bf16[1536,2304]{0,1:T(8,128)(2,1)} %all-gather.7.cloned.1.call-done, bf16[1,256,1536]{2,1,0:T(8,128)(2,1)S(1)} %copy-done.2, f32[1536]{0:T(1024)S(1)} %get-tuple-element.16, f32[1536]{0:T(1024)S(1)} %get-tuple-element.17, f32[256]{0:T(256)S(1)} %add_rsqrt_fusion.1, ...), kind=kOutput, calls=%fused_computation.10 | convolution fusion | flops 1814888448 | bytes 9058304 | tf_op jit(solution)/shard_map/dot_general | solution.py:131
  66.7 1.0 fusion.69
  67.7 0.0 all-gather.11.cloned.1.call-start
  67.8 0.5 all-gather.11.cloned.1.call-update
  69.0 0.1 select_reduce_fusion
  69.1 0.1 convert_reduce_fusion.1
  69.3 0.3 fusion.30
  70.3 1.0 copy.78
  71.4 31.0 %all-gather.5.cloned.1.call-done = bf16[1536,1536]{0,1:T(8,128)(2,1)} async-done(((bf16[1536,192]{0,1:T(8,128)(2,1)}), bf16[1536,1536]{0,1:T(8,128)(2,1)}) %all-gather.5.cloned.1.call-update) | async-done | bytes 4718608 | tf_op jit(solution)/shard_map/all_gather | solution.py:135
  102.3 4.0 %convolution_convert_fusion.1 = bf16[154,1536]{1,0:T(8,128)(2,1)S(1)} fusion(bf16[1536,1536]{0,1:T(8,128)(2,1)} %all-gather.5.cloned.1.call-done, bf16[1,154,1536]{2,1,0:T(8,128)(2,1)S(1)} %copy-done.4, f32[1536]{0:T(1024)S(1)} %get-tuple-element.18, f32[1536]{0:T(1024)S(1)} %get-tuple-element.19, f32[154]{0:T(256)S(1)} %add_rsqrt_fusion.2, ...), kind=kOutput, calls=%fused_computation.13 | convolution fusion | flops 728318976 | bytes 5678288 | tf_op jit(solution)/shard_map/dot_general | solution.py:134
  106.4 1.5 collective-permute-start
  108.0 0.9 copy.69
  108.9 0.9 copy.68
  109.8 2.3 %collective-permute-start.1 = (bf16[256,768]{1,0:T(8,128)(2,1)}, bf16[256,768]{1,0:T(8,128)(2,1)}, u32[]{:S(2)}, u32[]{:S(2)}) collective-permute-start(bf16[256,768]{1,0:T(8,128)(2,1)} %get-tuple-element.28), channel_id=1, source_target_pairs={{0,3},{1,0},{2,1},{3,2},{4,7},{5,4},{6,5},{7,6},{8,11},{9,8},{10,9... | collective-permute-start | bytes 1179656 | tf_op jit(solution)/shard_map/ppermute | solution.py:166
  112.2 0.2 copy.70
  112.3 1.6 bitcast_reduce_fusion.1
  113.9 10.9 %collective-permute-done = bf16[256,768]{1,0:T(8,128)(2,1)} collective-permute-done((bf16[256,768]{1,0:T(8,128)(2,1)}, bf16[256,768]{1,0:T(8,128)(2,1)}, u32[]{:S(2)}, u32[]{:S(2)}) %collective-permute-start) | collective-permute-done | bytes 393248 | tf_op jit(solution)/shard_map/ppermute | solution.py:161
  124.8 9.6 %collective-permute-start.2 = (bf16[256,768]{1,0:T(8,128)(2,1)}, bf16[256,768]{1,0:T(8,128)(2,1)}, u32[]{:S(2)}, u32[]{:S(2)}) collective-permute-start(bf16[256,768]{1,0:T(8,128)(2,1)} %collective-permute-done), channel_id=1, source_target_pairs={{0,1},{1,2},{2,3},{3,0},{4,5},{5,6},{6,7},{7,4},{8,9},{9,10},{10,1... | collective-permute-start | bytes 1179656 | tf_op jit(solution)/shard_map/ppermute | solution.py:161
  134.4 0.6 fusion.18
  134.9 1.9 copy.71
  136.9 1.3 broadcast_in_dim.83
  138.2 1.8 constant_dynamic-update-slice_fusion.2
  140.0 1.9 copy.72
  142.0 7.8 %collective-permute-done.1 = bf16[256,768]{1,0:T(8,128)(2,1)} collective-permute-done((bf16[256,768]{1,0:T(8,128)(2,1)}, bf16[256,768]{1,0:T(8,128)(2,1)}, u32[]{:S(2)}, u32[]{:S(2)}) %collective-permute-start.1) | collective-permute-done | bytes 393248 | tf_op jit(solution)/shard_map/ppermute | solution.py:166
  149.8 1.9 copy.73
  151.7 1.8 constant_dynamic-update-slice_fusion.1
  153.5 1.8 constant_dynamic-update-slice_fusion
  155.3 2.6 %collective-permute-done.2 = bf16[256,768]{1,0:T(8,128)(2,1)} collective-permute-done((bf16[256,768]{1,0:T(8,128)(2,1)}, bf16[256,768]{1,0:T(8,128)(2,1)}, u32[]{:S(2)}, u32[]{:S(2)}) %collective-permute-start.2) | collective-permute-done | bytes 393248 | tf_op jit(solution)/shard_map/ppermute | solution.py:161
  157.9 1.9 copy.74
  159.8 1.8 constant_dynamic-update-slice_fusion.3
  161.6 4.2 %bitcast_reduce_fusion = (f32[256,12]{0,1:T(8,128)S(1)}, f32[12,1024,256]{2,1,0:T(8,128)S(1)}) fusion(pred[1024]{0:T(1024)(128)(4,1)S(1)} %broadcast_compare_fusion, bf16[1024,12,64]{0,2,1:T(8,128)(2,1)} %bitcast.9, bf16[256,12,64]{0,2,1:T(8,128)(2,1)S(1)} %bitcast.133), kind=kOutput, calls=%fused_computation.1 | convolution fusion | flops 412087296 | bytes 14562304 | tf_op jit(solution)/shard_map/qhd,khd->qhk/dot_general | solution.py:89
  165.8 3.6 %fusion.2 = f32[256,12]{0,1:T(8,128)S(1)} fusion(f32[12,1024,256]{2,1,0:T(8,128)S(1)} %get-tuple-element.45, f32[256,12]{0,1:T(8,128)S(1)} %max.13, pred[1024]{0:T(1024)(128)(4,1)S(1)} %broadcast_compare_fusion), kind=kLoop, calls=%fused_computation.5 | loop fusion | flops 15725568 | bytes 12608512 | tf_op jit(solution)/shard_map/reduce_sum | solution.py:101
  169.4 1.0 copy-done.1
  170.4 0.0 all-gather.9.cloned.1.call-done
  170.4 2.6 %copy.75 = bf16[1024,768]{0,1:T(8,128)(2,1)} copy(bf16[1024,768]{1,0:T(8,128)(2,1)} %all-gather.9.cloned.1.call-done) | data formatting | bytes 3145728 | tf_op jit(solution)/shard_map/all_gather | solution.py:171
  173.0 7.8 %fusion.20 = f32[256,12,64]{0,2,1:T(8,128)S(1)} fusion(bf16[1024,12,64]{0,2,1:T(8,128)(2,1)} %bitcast.134, f32[12,1024,256]{2,1,0:T(8,128)} %copy-done.1, f32[256,12]{0,1:T(8,128)S(1)} %max.13, pred[1024]{0:T(1024)(128)(4,1)S(1)} %broadcast_compare_fusion), kind=kOutput, calls=%fused_computation.33 | convolution fusion | flops 418381824 | bytes 14955520 | tf_op jit(solution)/shard_map/qhk,khd->qhd/dot_general | solution.py:96
  180.9 0.7 fusion.26
  181.5 9.4 %all-gather.11.cloned.1.call-done = bf16[768,1536]{1,0:T(8,128)(2,1)} async-done(((bf16[96,1536]{1,0:T(8,128)(2,1)}), bf16[768,1536]{1,0:T(8,128)(2,1)}) %all-gather.11.cloned.1.call-update) | async-done | bytes 2359312 | tf_op jit(solution)/shard_map/all_gather | solution.py:184
  190.9 2.5 %fusion.72 = (f32[256]{0:T(256)S(1)}, f32[256,1536]{1,0:T(8,128)S(1)}) fusion(bf16[256,768]{0,1:T(8,128)(2,1)S(1)} %bitcast.136, bf16[768,1536]{1,0:T(8,128)(2,1)} %all-gather.11.cloned.1.call-done, f32[1536]{0:T(1024)S(1)} %get-tuple-element.20, bf16[1,256,1536]{2,1,0:T(8,128)(2,1)S(1)} %copy-done.2), kind=kOutput, calls=%fused_computation.131 | convolution fusion | flops 605552384 | bytes 5118976 | tf_op jit(solution)/shard_map/dot_general | solution.py:182
  193.5 0.3 multiply_reduce_fusion
  193.8 0.5 fusion.46
  194.3 0.1 reshape.190
  194.4 0.3 copy.77
  194.7 0.1 add_convert_fusion.2
  194.8 3.4 %collective-permute-start.3 = (bf16[1,16,1,128]{1,3,2,0:T(8,128)(2,1)S(1)}, bf16[1,16,1,128]{1,3,2,0:T(8,128)(2,1)S(1)}, u32[]{:S(2)}, u32[]{:S(2)}) collective-permute-start(bf16[1,16,1,128]{1,3,2,0:T(8,128)(2,1)S(1)} %get-tuple-element.31), channel_id=1, source_target_pairs={{0,1},{1,2},{2,3},{4,5},{5,6},{6,7},{8,9},{9,10},{10,11},{12,13},{... | collective-permute-start | bytes 12296 | tf_op jit(solution)/shard_map/ppermute | solution.py:24
  198.2 1.3 collective-permute-start.4
  199.5 0.1 copy.80
  199.6 0.8 copy.91
  200.4 0.8 copy.92
  201.2 0.1 copy.79
  201.3 2.7 %collective-permute-done.4 = bf16[1,16,1,128]{1,3,2,0:T(8,128)(2,1)S(1)} collective-permute-done((bf16[1,16,1,128]{1,3,2,0:T(8,128)(2,1)S(1)}, bf16[1,16,1,128]{1,3,2,0:T(8,128)(2,1)S(1)}, u32[]{:S(2)}, u32[]{:S(2)}) %collective-permute-start.4) | collective-permute-done | bytes 4128 | tf_op jit(solution)/shard_map/ppermute | solution.py:27
  204.0 0.1 copy.81
  204.1 0.1 fusion.59
  204.5 0.5 convolution_convert_fusion.2
  205.0 1.5 copy.93
  (42 shorter events, 0.4 us)
Async XLA Ops:
  7.2 186.6 %copy-start = (bf16[1536,64]{0,1:T(8,128)(2,1)S(1)}, bf16[1536,64]{0,1:T(8,128)(2,1)}, u32[]{:S(2)}) copy-start(bf16[1536,64]{0,1:T(8,128)(2,1)} %param.18) | copy-start | bytes 589828
  7.2 2.5 %copy-start.2 = (bf16[1,256,1536]{2,1,0:T(8,128)(2,1)S(1)}, bf16[1,256,1536]{2,1,0:T(8,128)(2,1)}, u32[]{:S(2)}) copy-start(bf16[1,256,1536]{2,1,0:T(8,128)(2,1)} %param.12) | copy-start | bytes 2359300
  7.2 54.3 %all-gather.7.cloned.1.call-start = ((), (), s32[]{:S(2)}) async-start(), calls=%async_computation.1 | async-start | bytes 7962624 | tf_op jit(solution)/shard_map/all_gather | solution.py:132
  7.9 94.4 %all-gather.5.cloned.1.call-start = ((), (), s32[]{:S(2)}) async-start(), calls=%async_computation | async-start | bytes 5308416 | tf_op jit(solution)/shard_map/all_gather | solution.py:135
  8.7 161.8 %all-gather.9.cloned.1.call-start = ((), (), s32[]{:S(2)}) async-start(), calls=%async_computation.2 | async-start | bytes 1966080 | tf_op jit(solution)/shard_map/all_gather | solution.py:171
  66.7 2.4 %copy-start.8 = (s32[1,1,4]{2,1,0:T(1,128)S(1)}, s32[1,1,4]{2,1,0:T(1,128)}, u32[]{:S(2)}) copy-start(s32[1,1,4]{2,1,0:T(1,128)} %param.20) | copy-start | bytes 52
  66.7 2.4 %copy-start.4 = (bf16[1,154,1536]{2,1,0:T(8,128)(2,1)S(1)}, bf16[1,154,1536]{2,1,0:T(8,128)(2,1)}, u32[]{:S(2)}) copy-start(bf16[1,154,1536]{2,1,0:T(8,128)(2,1)} %param.13) | copy-start | bytes 1419268
  66.7 3.6 %copy-start.7 = (f32[1,16,8,128]{3,2,1,0:T(8,128)S(1)}, f32[1,16,8,128]{3,2,1,0:T(8,128)}, u32[]{:S(2)}) copy-start(f32[1,16,8,128]{3,2,1,0:T(8,128)} %param.22) | copy-start | bytes 196612
  67.7 123.2 %all-gather.11.cloned.1.call-start = ((), (), s32[]{:S(2)}) async-start(), calls=%async_computation.3 | async-start | bytes 2654208 | tf_op jit(solution)/shard_map/all_gather | solution.py:184
  106.4 18.4 %collective-permute-start = (bf16[256,768]{1,0:T(8,128)(2,1)}, bf16[256,768]{1,0:T(8,128)(2,1)}, u32[]{:S(2)}, u32[]{:S(2)}) collective-permute-start(bf16[256,768]{1,0:T(8,128)(2,1)} %get-tuple-element.28), channel_id=1, source_target_pairs={{0,1},{1,2},{2,3},{3,0},{4,5},{5,6},{6,7},{7,4},{8,9},{9,10},{10,1... | collective-permute-start | bytes 1179656 | tf_op jit(solution)/shard_map/ppermute | solution.py:161
  109.8 39.9 %collective-permute-start.1 = (bf16[256,768]{1,0:T(8,128)(2,1)}, bf16[256,768]{1,0:T(8,128)(2,1)}, u32[]{:S(2)}, u32[]{:S(2)}) collective-permute-start(bf16[256,768]{1,0:T(8,128)(2,1)} %get-tuple-element.28), channel_id=1, source_target_pairs={{0,3},{1,0},{2,1},{3,2},{4,7},{5,4},{6,5},{7,6},{8,11},{9,8},{10,9... | collective-permute-start | bytes 1179656 | tf_op jit(solution)/shard_map/ppermute | solution.py:166
  124.8 33.1 %collective-permute-start.2 = (bf16[256,768]{1,0:T(8,128)(2,1)}, bf16[256,768]{1,0:T(8,128)(2,1)}, u32[]{:S(2)}, u32[]{:S(2)}) collective-permute-start(bf16[256,768]{1,0:T(8,128)(2,1)} %collective-permute-done), channel_id=1, source_target_pairs={{0,1},{1,2},{2,3},{3,0},{4,5},{5,6},{6,7},{7,4},{8,9},{9,10},{10,1... | collective-permute-start | bytes 1179656 | tf_op jit(solution)/shard_map/ppermute | solution.py:161
  165.8 4.6 %copy-start.1 = (f32[12,1024,256]{2,1,0:T(8,128)}, f32[12,1024,256]{2,1,0:T(8,128)S(1)}, u32[]{:S(2)}) copy-start(f32[12,1024,256]{2,1,0:T(8,128)S(1)} %get-tuple-element.45) | copy-start | bytes 37748740
  173.0 7.8 %copy-start.5 = (bf16[154,768]{0,1:T(8,128)(2,1)S(1)}, bf16[154,768]{0,1:T(8,128)(2,1)}, u32[]{:S(2)}) copy-start(bf16[154,768]{0,1:T(8,128)(2,1)} %copy.68) | copy-start | bytes 709636
  193.5 1.2 copy-start.3
  194.7 9.8 %copy-start.6 = (bf16[512,144]{0,1:T(8,128)(2,1)S(1)}, bf16[512,144]{0,1:T(8,128)(2,1)}, u32[]{:S(2)}) copy-start(bf16[512,144]{0,1:T(8,128)(2,1)} %param.23) | copy-start | bytes 442372
  194.8 6.4 %collective-permute-start.3 = (bf16[1,16,1,128]{1,3,2,0:T(8,128)(2,1)S(1)}, bf16[1,16,1,128]{1,3,2,0:T(8,128)(2,1)S(1)}, u32[]{:S(2)}, u32[]{:S(2)}) collective-permute-start(bf16[1,16,1,128]{1,3,2,0:T(8,128)(2,1)S(1)} %get-tuple-element.31), channel_id=1, source_target_pairs={{0,1},{1,2},{2,3},{4,5},{5,6},{6,7},{8,9},{9,10},{10,11},{12,13},{... | collective-permute-start | bytes 12296 | tf_op jit(solution)/shard_map/ppermute | solution.py:24
  198.2 5.8 %collective-permute-start.4 = (bf16[1,16,1,128]{1,3,2,0:T(8,128)(2,1)S(1)}, bf16[1,16,1,128]{1,3,2,0:T(8,128)(2,1)S(1)}, u32[]{:S(2)}, u32[]{:S(2)}) collective-permute-start(bf16[1,16,1,128]{1,3,2,0:T(8,128)(2,1)S(1)} %get-tuple-element.32), channel_id=1, source_target_pairs={{1,0},{2,1},{3,2},{5,4},{6,5},{7,6},{9,8},{10,9},{11,10},{13,12},{... | collective-permute-start | bytes 12296 | tf_op jit(solution)/shard_map/ppermute | solution.py:27
Sparse Core Ops, SparseCore 0:
  9.9 51.5 all-gather.6
  63.4 38.9 all-gather.4
  103.9 58.2 all-gather.8
  164.0 26.8 all-gather.10
